TPU v7x, 512 devices: a whole 4x8x8 slice. The times are simulated.
512 devices in a mesh: dp: 8 (over y), fsdp: 64 (over x, z, core).
Axes of the slice: x: 4, y: 8, z: 8, core: 2. Of those that a mesh axis runs over, the one named last changes fastest.
Arguments:
- q_pre: bfloat16 [8, 8192, 3072], P('dp', 'fsdp'), may hold values from -8 to 8
- k_pre: bfloat16 [8, 8192, 3072], P('dp', 'fsdp'), may hold values from -8 to 8
- values: bfloat16 [8, 8192, 3072], P('dp', 'fsdp'), may hold values from -6 to 6
- grad_out: bfloat16 [8, 8192, 3072], P('dp', 'fsdp'), may hold values from -6 to 6
- segment_ids: int32 [8, 8192], P('dp', 'fsdp'), may hold values from 0 to 127, never falling along the last dimension, each value on 1 to 128 neighbouring positions
- gain_q: float32 [24, 128], replicated, may hold values from 0.5 to 4.5
- gain_k: float32 [24, 128], replicated, may hold values from 0.5 to 4.5
Outputs:
- grad_q_pre: bfloat16 [8, 8192, 3072], P('dp', 'fsdp')
- grad_k_pre: bfloat16 [8, 8192, 3072], P('dp', 'fsdp')
- grad_gain_q: float32 [24, 128], replicated
- grad_gain_k: float32 [24, 128], replicated
Inputs may be any that keep to these rules, and one draw needn't show every extreme that they name: `segment_ids`: in each group, ids never fall along the positions; every image covers 1 to 128 positions, and one covers exactly 128.
All inputs are finite; a program needn't handle non-finite values.
Results may differ from a plain program's by a relative error of at most 0.011.
The roundings to bfloat16 on the way count: a program that leaves them out, or rounds other values in their place, can miss the bound.
Values may be sent and summed in bfloat16 or wider, within the bound.
A program may use at most 64 MiB of HBM per device.

v0:
```python
import jax
import jax.numpy as jnp
from jax import lax
from jax.sharding import PartitionSpec as P


def from_behind(block, axis, distance):
    devices = range(lax.axis_size(axis))
    route = [(i - distance, i) for i in devices if i - distance in devices]
    return lax.ppermute(block, axis, route)


def layer_norm(x, gain):
    mean = jnp.mean(x, -1, keepdims=True)
    centered = x - mean
    var = jnp.mean(centered * centered, -1, keepdims=True)
    return centered * lax.rsqrt(var + 1e-06) * gain


def head_major(x):
    return jnp.transpose(x, (1, 0, 2))


def attend(queries, cotangent, keys, vals, row_ids, scale):
    match = row_ids[:, None] == row_ids[None, :]

    def one_head(items):
        q_head, c_head, k_head, v_head = items
        scores = jnp.dot(q_head, k_head.T, preferred_element_type=jnp.float32) * scale
        masked = jnp.where(match, scores, jnp.float32(-1e30))
        top = jnp.max(masked, -1, keepdims=True)
        expo = jnp.where(match, jnp.exp(masked - top), jnp.float32(0.0))
        total = jnp.sum(expo, -1, keepdims=True)
        probs = expo / total
        dprob = jnp.dot(c_head, v_head.T, preferred_element_type=jnp.float32)
        delta = jnp.sum(probs * dprob, -1, keepdims=True)
        slopes = (probs * (dprob - delta) * scale).astype(jnp.bfloat16)
        dq_head = jnp.dot(slopes, k_head, preferred_element_type=jnp.float32)
        dk_head = jnp.dot(slopes.T, q_head, preferred_element_type=jnp.float32)
        return (dq_head, dk_head)

    dq_all, dk_all = lax.map(
        one_head, (head_major(queries), head_major(cotangent), head_major(keys), head_major(vals))
    )
    return (head_major(dq_all), head_major(dk_all))


def per_device(q_pre, k_pre, values, grad_out, segment_ids, gain_q, gain_k):
    heads, depth = gain_q.shape
    rows = q_pre.shape[1]
    width = heads * depth
    scale = depth ** (-0.5)
    own_ids = segment_ids[0] + 1
    prior = from_behind(own_ids, "fsdp", 1)
    later = from_behind(own_ids, "fsdp", -1)
    given = own_ids == prior[rows - 1]
    taken = later == own_ids[rows - 1]
    buffer_ids = jnp.concatenate([jnp.where(given, -1, own_ids), jnp.where(taken, later, -2)])
    q_float = q_pre[0].astype(jnp.float32).reshape(rows, heads, depth)
    k_float = k_pre[0].astype(jnp.float32).reshape(rows, heads, depth)
    q_normed, q_back = jax.vjp(layer_norm, q_float, gain_q)
    k_normed, k_back = jax.vjp(layer_norm, k_float, gain_k)
    q_half = q_normed.astype(jnp.bfloat16)
    k_half = k_normed.astype(jnp.bfloat16)
    own_values = values[0].reshape(rows, heads, depth)
    own_cotangent = grad_out[0].reshape(rows, heads, depth)
    given_rows = given[:, None, None]
    sent = jnp.stack(
        [q_half.reshape(rows, width), k_half.reshape(rows, width), values[0], grad_out[0]]
    )
    far = from_behind(sent, "fsdp", -1).reshape(4, rows, heads, depth)
    queries = jnp.concatenate([q_half, far[0]])
    keys = jnp.concatenate([k_half, far[1]])
    vals = jnp.concatenate([own_values, far[2]])
    cotangent = jnp.concatenate([own_cotangent, far[3]])
    dq_buf, dk_buf = attend(queries, cotangent, keys, vals, buffer_ids, scale)
    back_q, back_k = (
        from_behind(dq_buf[rows:].astype(jnp.bfloat16), "fsdp", 1).astype(jnp.float32),
        from_behind(dk_buf[rows:].astype(jnp.bfloat16), "fsdp", 1).astype(jnp.float32),
    )
    grad_q = jnp.where(given_rows, back_q, dq_buf[:rows])
    grad_k = jnp.where(given_rows, back_k, dk_buf[:rows])
    dq_pre, dgain_q = q_back(grad_q)
    dk_pre, dgain_k = k_back(grad_k)
    out_q = dq_pre.reshape(rows, width).astype(jnp.bfloat16)
    out_k = dk_pre.reshape(rows, width).astype(jnp.bfloat16)
    total_q, total_k = lax.psum((dgain_q, dgain_k), ("dp", "fsdp"))
    return (out_q.reshape(1, rows, width), out_k.reshape(1, rows, width), total_q, total_k)


def solution(mesh):
    return jax.shard_map(
        per_device,
        mesh=mesh,
        in_specs=(
            P("dp", "fsdp", None),
            P("dp", "fsdp", None),
            P("dp", "fsdp", None),
            P("dp", "fsdp", None),
            P("dp", "fsdp"),
            P(),
            P(),
        ),
        out_specs=(P("dp", "fsdp", None), P("dp", "fsdp", None), P(), P()),
        check_vma=False,
    )
```

profile of v0, /device:TPU:1, one launch (start us, length us, event | category | flops | bytes accessed | tf_op | source)
XLA Modules:
  0.0 342.4 jit_solution(14804321148009965187)
XLA Ops:
  8.8 1.9 pad_maximum_fusion
  10.7 8.8 %collective-permute-start.1 = (bf16[4,128,3072]{1,2,0:T(8,128)(2,1)}, bf16[4,128,3072]{1,2,0:T(8,128)(2,1)}, u32[]{:S(2)}, u32[]{:S(2)}) collective-permute-start(bf16[4,128,3072]{1,2,0:T(8,128)(2,1)} %pad_maximum_fusion), channel_id=1, source_target_pairs={{1,0},{2,1},{3,2},{4,3},{5,4},{6,5},{7,6},{8,7},{9,8},{10,9},{11,1... | collective-permute-start | bytes 9437192 | tf_op jit(solution)/shard_map/ppermute | solution.py:10
  19.5 1.9 collective-permute-start.2
  21.4 3.6 %collective-permute-start = (s32[128]{0:T(128)S(1)}, s32[128]{0:T(128)S(1)}, u32[]{:S(2)}, u32[]{:S(2)}) collective-permute-start(s32[128]{0:T(128)S(1)} %get-tuple-element.121), channel_id=1, source_target_pairs={{0,1},{1,2},{2,3},{3,4},{4,5},{5,6},{6,7},{7,8},{8,9},{9,10},{10,1... | collective-permute-start | bytes 1544 | tf_op jit(solution)/shard_map/ppermute | solution.py:10
  29.7 21.6 %collective-permute-done.2 = s32[128]{0:T(128)S(1)} collective-permute-done((s32[128]{0:T(128)S(1)}, s32[128]{0:T(128)S(1)}, u32[]{:S(2)}, u32[]{:S(2)}) %collective-permute-start.2) | collective-permute-done | bytes 544 | tf_op jit(solution)/shard_map/ppermute | solution.py:10
  52.0 2.1 fusion.34
  59.7 140.7 %while.13 = (s32[]{:T(128)}, f32[24,256,128]{1,2,0:T(8,128)}, f32[24,256,128]{1,2,0:T(8,128)}, bf16[24,256,128]{1,2,0:T(8,128)(2,1)}, bf16[24,256,128]{1,2,0:T(8...) while((s32[]{:T(128)}, f32[24,256,128]{1,2,0:T(8,128)}, ...), condition=%wide.region_8.9_spmd.clone, body=%wide.region_4.8_spmd.clone.sunk | while | flops 68549888 | bytes 2640997 | solution.py:42
  73.9 1.7 fusion.52
  103.2 1.7 fusion.52
  120.8 1.7 fusion.52
  126.6 1.7 fusion.52
  132.5 1.7 fusion.52
  138.4 1.7 fusion.52
  144.2 1.7 fusion.52
  150.1 1.7 fusion.52
  161.8 1.7 fusion.52
  167.7 1.7 fusion.52
  173.6 1.7 fusion.52
  179.4 1.7 fusion.52
  185.3 1.7 fusion.52
  191.2 1.7 fusion.52
  197.0 1.7 fusion.52
  200.4 1.7 slice.80
  203.6 1.9 collective-permute-start.4
  205.6 4.4 %collective-permute-start.3 = (bf16[128,24,128]{0,2,1:T(8,128)(2,1)S(1)}, bf16[128,24,128]{0,2,1:T(8,128)(2,1)S(1)}, u32[]{:S(2)}, u32[]{:S(2)}) collective-permute-start(bf16[128,24,128]{0,2,1:T(8,128)(2,1)S(1)} %slice.80), channel_id=1, source_target_pairs={{0,1},{1,2},{2,3},{3,4},{4,5},{5,6},{6,7},{7,8},{8,9},{9,10},{10,1... | collective-permute-start | bytes 2359304 | tf_op jit(solution)/shard_map/ppermute | solution.py:10
  210.6 3.9 %collective-permute-done.4 = bf16[128,24,128]{0,2,1:T(8,128)(2,1)S(1)} collective-permute-done((bf16[128,24,128]{0,2,1:T(8,128)(2,1)S(1)}, bf16[128,24,128]{0,2,1:T(8,128)(2,1)S(1)}, u32[]{:S(2)}, u32[]{:S(2)}) %collective-permute-start.4) | collective-permute-done | bytes 786464 | tf_op jit(solution)/shard_map/ppermute | solution.py:10
  214.5 8.4 %collective-permute-done.3 = bf16[128,24,128]{0,2,1:T(8,128)(2,1)S(1)} collective-permute-done((bf16[128,24,128]{0,2,1:T(8,128)(2,1)S(1)}, bf16[128,24,128]{0,2,1:T(8,128)(2,1)S(1)}, u32[]{:S(2)}, u32[]{:S(2)}) %collective-permute-start.3) | collective-permute-done | bytes 786464 | tf_op jit(solution)/shard_map/ppermute | solution.py:10
  222.9 2.4 multiply_reduce_fusion.3
  225.4 2.7 multiply_reduce_fusion.1
  228.1 2.7 add_convert_fusion
  230.8 2.4 copy.26
  234.3 108.0 %all-reduce = (f32[24,128]{1,0:T(8,128)}, f32[24,128]{1,0:T(8,128)}) all-reduce(f32[24,128]{1,0:T(8,128)S(1)} %get-tuple-element.85, f32[24,128]{1,0:T(8,128)S(1)} %get-tuple-element.80), channel_id=1, replica_groups=mesh['dp'=8,'fsdp'=64] {'dp','fsdp'}, use_global_device_ids=true, to_apply=%region_14.15 | all-reduce | flops 6144 | bytes 49152 | tf_op jit(solution)/shard_map/psum | solution.py:87
  (203 shorter events, 137.1 us)
Async XLA Ops:
  0.6 1.8 copy-start.13
  2.2 0.9 copy-start
  2.2 1.4 copy-start.14
  2.8 3.2 copy-start.2
  2.8 2.0 copy-start.15
  6.0 1.1 copy-start.1
  6.2 1.2 copy-start.3
  6.2 1.2 copy-start.16
  6.3 1.2 copy-start.17
  7.4 1.1 copy-start.6
  7.4 1.4 copy-start.8
  8.8 10.7 %copy-start.18 = (s32[1,128]{1,0:T(1,128)S(1)}, s32[1,128]{1,0:T(1,128)}, u32[]{:S(2)}) copy-start(s32[1,128]{1,0:T(1,128)} %param.13) | copy-start | bytes 1540
  10.7 41.3 %collective-permute-start.1 = (bf16[4,128,3072]{1,2,0:T(8,128)(2,1)}, bf16[4,128,3072]{1,2,0:T(8,128)(2,1)}, u32[]{:S(2)}, u32[]{:S(2)}) collective-permute-start(bf16[4,128,3072]{1,2,0:T(8,128)(2,1)} %pad_maximum_fusion), channel_id=1, source_target_pairs={{1,0},{2,1},{3,2},{4,3},{5,4},{6,5},{7,6},{8,7},{9,8},{10,9},{11,1... | collective-permute-start | bytes 9437192 | tf_op jit(solution)/shard_map/ppermute | solution.py:10
  19.5 31.8 %collective-permute-start.2 = (s32[128]{0:T(128)S(1)}, s32[128]{0:T(128)S(1)}, u32[]{:S(2)}, u32[]{:S(2)}) collective-permute-start(s32[128]{0:T(128)S(1)} %get-tuple-element.121), channel_id=1, source_target_pairs={{1,0},{2,1},{3,2},{4,3},{5,4},{6,5},{7,6},{8,7},{9,8},{10,9},{11,1... | collective-permute-start | bytes 1544 | tf_op jit(solution)/shard_map/ppermute | solution.py:10
  21.4 7.0 %collective-permute-start = (s32[128]{0:T(128)S(1)}, s32[128]{0:T(128)S(1)}, u32[]{:S(2)}, u32[]{:S(2)}) collective-permute-start(s32[128]{0:T(128)S(1)} %get-tuple-element.121), channel_id=1, source_target_pairs={{0,1},{1,2},{2,3},{3,4},{4,5},{5,6},{6,7},{7,8},{8,9},{9,10},{10,1... | collective-permute-start | bytes 1544 | tf_op jit(solution)/shard_map/ppermute | solution.py:10
  52.0 2.2 copy-start.9
  54.2 1.5 copy-start.7
  55.6 1.3 copy-start.11
  57.0 1.4 copy-start.10
  200.4 22.5 %copy-start.4 = (f32[24,256,128]{1,2,0:T(8,128)S(1)}, f32[24,256,128]{1,2,0:T(8,128)}, u32[]{:S(2)}) copy-start(f32[24,256,128]{1,2,0:T(8,128)} %get-tuple-element.48) | copy-start | bytes 9437188
  203.6 10.8 %collective-permute-start.4 = (bf16[128,24,128]{0,2,1:T(8,128)(2,1)S(1)}, bf16[128,24,128]{0,2,1:T(8,128)(2,1)S(1)}, u32[]{:S(2)}, u32[]{:S(2)}) collective-permute-start(bf16[128,24,128]{0,2,1:T(8,128)(2,1)S(1)} %slice.79), channel_id=1, source_target_pairs={{0,1},{1,2},{2,3},{3,4},{4,5},{5,6},{6,7},{7,8},{8,9},{9,10},{10,1... | collective-permute-start | bytes 2359304 | tf_op jit(solution)/shard_map/ppermute | solution.py:10
  205.6 17.3 %collective-permute-start.3 = (bf16[128,24,128]{0,2,1:T(8,128)(2,1)S(1)}, bf16[128,24,128]{0,2,1:T(8,128)(2,1)S(1)}, u32[]{:S(2)}, u32[]{:S(2)}) collective-permute-start(bf16[128,24,128]{0,2,1:T(8,128)(2,1)S(1)} %slice.80), channel_id=1, source_target_pairs={{0,1},{1,2},{2,3},{3,4},{4,5},{5,6},{6,7},{7,8},{8,9},{9,10},{10,1... | collective-permute-start | bytes 2359304 | tf_op jit(solution)/shard_map/ppermute | solution.py:10
  210.6 14.8 %copy-start.5 = (f32[24,256,128]{1,2,0:T(8,128)S(1)}, f32[24,256,128]{1,2,0:T(8,128)}, u32[]{:S(2)}) copy-start(f32[24,256,128]{1,2,0:T(8,128)} %get-tuple-element.47) | copy-start | bytes 9437188
  230.8 2.4 copy-start.12
where the time goes:
time: 347 us; the launch traced here: 342 us
  matrix products  134 us (39%)
  blocking collectives  108 us (31%)
  waiting for transfers between devices  33.9 us (10%)
  other arithmetic  27.7 us (8%)
  starting transfers between devices  20.6 us (6%)
  local copies, waits for them, and re-layouts  16.3 us (5%)
    psum x1, blocking collectives, per_device(): total_q, total_k = lax.psum((dgain_q, dgain_k), ('dp', 'fsdp'))  108 us
    dot_general x24, matrix products, one_head(): dk_head = jnp.dot(slopes.T, q_head, preferred_element_type=jnp.float32)  40.6 us
    dot_general x24, matrix products, one_head(): dq_head = jnp.dot(slopes, k_head, preferred_element_type=jnp.float32)  39.7 us
    ppermute x5, waiting for transfers between devices, from_behind(): return lax.ppermute(block, axis, route)  33.9 us
    dot_general x24, matrix products, one_head(): dprob = jnp.dot(c_head, v_head.T, preferred_element_type=jnp.float32)  27.1 us
    dot_general x24, matrix products, one_head(): jnp.dot(q_head, k_head.T, preferred_element_type=jnp.float32) * scale  27 us
    ppermute x5, starting transfers between devices, from_behind(): return lax.ppermute(block, axis, route)  20.6 us
    unnamed x44, local copies, waits for them, and re-layouts  9.73 us
  transfers between devices with their start and end apart: 5, of which 3 were waited for; matrix products, arithmetic and copies ran while one was open for 2% of the time, Pallas kernels for 0%

commit v1 on v0

v1 whole, which is shorter than its diff:
```python
import math

import jax
import jax.numpy as jnp
from jax import lax
from jax.experimental import pallas as pl
from jax.experimental.pallas import tpu as pltpu
from jax.sharding import PartitionSpec as P

MESH = pl.DeviceIdType.MESH
F32 = jnp.float32
BF16 = jnp.bfloat16

HEADS = 24
DEPTH = 128
ROWS = 128
HALF = ROWS // 2
WIDTH = HEADS * DEPTH
PER_STEP = 2
STEPS = HEADS // PER_STEP
COLS = PER_STEP * DEPTH
SCALE = DEPTH**-0.5
SCALE_LOG2 = SCALE * math.log2(math.e)


def dot(a, b, contract_a, contract_b):
    dims = (((contract_a,), (contract_b,)), ((), ()))
    return lax.dot_general(a, b, dims, preferred_element_type=F32)


def lane_mean(x):
    return jnp.sum(x, -1, keepdims=True) * (1.0 / DEPTH)


def normalize(x, gain):
    centered = x - lane_mean(x)
    inverse = lax.rsqrt(lane_mean(centered * centered) + 1e-06)
    unit = centered * inverse
    return unit, inverse, (unit * gain).astype(BF16)


def normalize_back(grad, unit, inverse, gain):
    d_unit = grad * gain
    mean = lane_mean(d_unit)
    slope = lane_mean(d_unit * unit)
    return (inverse * (d_unit - mean - unit * slope)).astype(BF16)


def attention_back(queries, keys, values, cotangent, bias):
    scores = dot(keys, queries, 1, 1) * SCALE_LOG2 + bias
    expo = jnp.exp2(scores - jnp.max(scores, 0, keepdims=True))
    total = jnp.sum(expo, 0, keepdims=True)
    dprob = dot(values, cotangent, 1, 1)
    delta = jnp.sum(expo * dprob, 0, keepdims=True) / total
    slopes = (expo * (SCALE / total) * (dprob - delta)).astype(BF16)
    return dot(slopes, keys, 0, 0), dot(slopes, queries, 1, 0)


def place():
    f = lax.axis_index("fsdp")
    return lax.axis_index("dp"), f // 16, lax.rem(f, 16) // 2, lax.rem(f, 2)


def groups():
    y, x, z, c = place()
    return {
        "core": (2, c, lambda j: {"fsdp": x * 16 + z * 2 + j}),
        "x": (4, x, lambda j: {"fsdp": j * 16 + z * 2 + c}),
        "y": (8, y, lambda j: {"dp": j}),
        "z": (8, z, lambda j: {"fsdp": x * 16 + j * 2 + c}),
    }


def greet(left, right):
    barrier = pltpu.get_barrier_semaphore()
    for device in (left, right):
        pl.semaphore_signal(barrier, inc=1, device_id=device, device_id_type=MESH)
    count = 2
    for size, me, member in groups().values():
        for i in range(1, size):
            peer = member(lax.rem(me + i, size))
            pl.semaphore_signal(barrier, inc=1, device_id=peer, device_id_type=MESH)
        count += size - 1
    return barrier, count


def kernel(
    q_ref, k_ref, v_ref, g_ref, ids_ref, gain_q_ref, gain_k_ref,
    out_q_ref, out_k_ref, sum_ref,
    own, halo, sent_back, came_back, result, gains, d_gains,
    ids_in, ids_own, ids_near, bias, weight, given,
    core_in, x_in, y_in, z_in, final,
    local_sem, id_send, id_recv, far_send, far_recv, back_send, back_recv,
    core_sem, x_sem, y_sem, z_sem, last_sem,
):
    f = lax.axis_index("fsdp")
    size = lax.axis_size("fsdp")
    left = {"fsdp": lax.rem(f + size - 1, size)}
    right = {"fsdp": lax.rem(f + 1, size)}
    barrier, count = greet(left, right)

    sources = (q_ref, k_ref, v_ref, g_ref)
    loads = [pltpu.make_async_copy(ids_ref, ids_in, local_sem.at[4])]
    loads += [pltpu.make_async_copy(s, own.at[i], local_sem.at[i]) for i, s in enumerate(sources)]
    loads += [
        pltpu.make_async_copy(gain_q_ref, gains.at[0], local_sem.at[5]),
        pltpu.make_async_copy(gain_k_ref, gains.at[1], local_sem.at[6]),
    ]
    for load in loads:
        load.start()
    loads[0].wait()
    ids_own[...] = jnp.broadcast_to(ids_in[...], (8, ROWS))
    pl.semaphore_wait(barrier, count)

    def id_copy(side):
        return pltpu.make_async_remote_copy(
            src_ref=ids_own, dst_ref=ids_near.at[side], send_sem=id_send.at[side], recv_sem=id_recv.at[side],
            device_id=(left, right)[side], device_id_type=MESH,
        )

    def far_copy(step, array, side):
        rows = pl.ds(side * HALF, HALF)
        columns = pl.ds(pl.multiple_of(step * COLS, COLS), COLS)
        return pltpu.make_async_remote_copy(
            src_ref=sources[array].at[rows, columns], dst_ref=halo.at[array, rows, columns],
            send_sem=far_send.at[side, array, step], recv_sem=far_recv.at[side, array, step],
            device_id=(left, right)[side], device_id_type=MESH,
        )

    def back_copy(step, array, side):
        rows = pl.ds(side * HALF, HALF)
        columns = pl.ds(pl.multiple_of(step * COLS, COLS), COLS)
        return pltpu.make_async_remote_copy(
            src_ref=sent_back.at[array, rows, columns], dst_ref=came_back.at[array, rows, columns],
            send_sem=back_send.at[side, array, step], recv_sem=back_recv.at[side, array, step],
            device_id=(right, left)[side], device_id_type=MESH,
        )

    for side in (0, 1):
        id_copy(side).start()

    def send_far(step, carry):
        for array in range(4):
            for side in (0, 1):
                far_copy(step, array, side).start()
        return carry

    lax.fori_loop(0, STEPS, send_far, 0)

    for side in (0, 1):
        id_copy(side).wait()
    mine = ids_own[0:1, :]
    after = jnp.where(f < size - 1, ids_near[0, 0:1, :], -2)
    before = jnp.where(f > 0, ids_near[1, 0:1, :], -2)
    lane = lax.broadcasted_iota(jnp.int32, (1, ROWS), 1)

    def pick(x, at):
        return jnp.sum(jnp.where(lane == at, x, 0), -1, keepdims=True)

    first, last = pick(mine, 0), pick(mine, ROWS - 1)
    tail_before, head_after = pick(before, ROWS - 1), pick(after, 0)
    half_before, half_mine = pick(before, HALF - 1), pick(mine, HALF - 1)
    in_left = mine == tail_before
    in_right = mine == head_after
    take_left = half_before != first
    take_right = half_mine == last
    low = lane < HALF
    use_right = low & (after == last) & take_right
    use_left = (~low) & (before == first) & take_left
    halo_ids = jnp.where(use_right | use_left, jnp.where(low, after, before), -1)
    given_row = ((in_left & ~take_left) | (in_right & ~take_right)).astype(F32)
    used_row = (use_right | use_left).astype(F32)
    ids_row = jnp.concatenate([mine, halo_ids], 1).astype(F32)
    across = jnp.broadcast_to(ids_row, (2 * ROWS, 2 * ROWS))
    bias[...] = jnp.where(across == across.T, 0.0, -1e30).astype(F32)
    weight_row = jnp.concatenate([1.0 - given_row, used_row], 1)
    weight[...] = jnp.broadcast_to(weight_row, (ROWS, 2 * ROWS)).T
    given[...] = jnp.broadcast_to(given_row, (ROWS, ROWS)).T

    for load in loads[1:]:
        load.wait()

    def compute(step, carry):
        for array in range(4):
            for side in (0, 1):
                far_copy(step, array, side).wait_recv()
        for part in range(PER_STEP):
            head = step * PER_STEP + part
            columns = pl.ds(pl.multiple_of(head * DEPTH, DEPTH), DEPTH)
            gain = [gains[i, pl.ds(head, 1), :] for i in range(2)]
            raw = [jnp.concatenate([own[i, :, columns], halo[i, :, columns]], 0) for i in range(4)]
            unit, inverse, normed = zip(*[normalize(raw[i].astype(F32), gain[i]) for i in range(2)])
            grads = attention_back(normed[0], normed[1], raw[2], raw[3], bias[...])
            for i in range(2):
                d_gains[i, pl.ds(head, 1), :] = jnp.sum(grads[i] * unit[i] * weight[...], 0, keepdims=True)
                d_raw = normalize_back(grads[i], unit[i], inverse[i], gain[i])
                result[i, :, columns] = d_raw[:ROWS]
                sent_back[i, :, columns] = d_raw[ROWS:]
        return carry

    lax.fori_loop(0, STEPS, compute, 0)

    def send_back(step, carry):
        for array in range(2):
            for side in (0, 1):
                back_copy(step, array, side).start()
        return carry

    lax.fori_loop(0, STEPS, send_back, 0)

    members = groups()
    core = members["core"][1]
    other = 1 - core

    def core_copy(source, target, pair):
        return pltpu.make_async_remote_copy(
            src_ref=source, dst_ref=target, send_sem=pair.at[0], recv_sem=pair.at[1],
            device_id=members["core"][2](other), device_id_type=MESH,
        )

    first_copy = core_copy(d_gains.at[other], core_in, core_sem)
    first_copy.start()
    first_copy.wait()

    def exchange(name, block, slots, sems):
        size, me, member = members[name]
        slots[me] = block
        copies = []
        for i in range(1, size):
            peer = lax.rem(me + i, size)
            copies.append(
                pltpu.make_async_remote_copy(
                    src_ref=slots.at[me], dst_ref=slots.at[me], send_sem=sems.at[0, i], recv_sem=sems.at[1, size - i],
                    device_id=member(peer), device_id_type=MESH,
                )
            )
        for copy in copies:
            copy.start()
        return copies

    def total(slots, copies):
        for copy in copies:
            copy.wait()
        return jnp.sum(slots[...], 0)

    copies = exchange("x", d_gains[core] + core_in[...], x_in, x_sem)
    copies = exchange("y", total(x_in, copies), y_in, y_sem)
    copies = exchange("z", total(y_in, copies), z_in, z_sem)

    def finish(step, carry):
        for array in range(2):
            for side in (0, 1):
                back_copy(step, array, side).wait_recv()
        for part in range(PER_STEP):
            columns = pl.ds(pl.multiple_of(step * COLS + part * DEPTH, DEPTH), DEPTH)
            away = given[...] != 0.0
            for i in range(2):
                mixed = jnp.where(away, came_back[i, :, columns].astype(F32), result[i, :, columns].astype(F32))
                result[i, :, columns] = mixed.astype(BF16)
        return carry

    lax.fori_loop(0, STEPS, finish, 0)
    stores = [
        pltpu.make_async_copy(result.at[i], out, local_sem.at[i]) for i, out in enumerate((out_q_ref, out_k_ref))
    ]
    for store in stores:
        store.start()
    final[core] = total(z_in, copies)
    last_copy = core_copy(final.at[core], final.at[core], last_sem)
    last_copy.start()
    last_copy.wait()
    sum_ref[...] = final[...]

    def drain(step, carry):
        for side in (0, 1):
            for array in range(4):
                far_copy(step, array, side).wait_send()
            for array in range(2):
                back_copy(step, array, side).wait_send()
        return carry

    lax.fori_loop(0, STEPS, drain, 0)
    for store in stores:
        store.wait()


def per_device(q_pre, k_pre, values, grad_out, segment_ids, gain_q, gain_k):
    anywhere = pl.BlockSpec(memory_space=pl.ANY)
    vmem, dma = pltpu.VMEM, pltpu.SemaphoreType.DMA
    wide = (ROWS, WIDTH)
    part = (HEADS, DEPTH)
    out_q, out_k, sums = pl.pallas_call(
        kernel,
        out_shape=[
            jax.ShapeDtypeStruct(wide, BF16),
            jax.ShapeDtypeStruct(wide, BF16),
            jax.ShapeDtypeStruct((2,) + part, F32),
        ],
        in_specs=[anywhere] * 7,
        out_specs=[anywhere, anywhere, pl.BlockSpec(memory_space=vmem)],
        scratch_shapes=[
            vmem((4,) + wide, BF16),
            vmem((4,) + wide, BF16),
            vmem((2,) + wide, BF16),
            vmem((2,) + wide, BF16),
            vmem((2,) + wide, BF16),
            vmem((2,) + part, F32),
            vmem((2,) + part, F32),
            vmem((1, ROWS), jnp.int32),
            vmem((8, ROWS), jnp.int32),
            vmem((2, 8, ROWS), jnp.int32),
            vmem((2 * ROWS, 2 * ROWS), F32),
            vmem((2 * ROWS, ROWS), F32),
            vmem((ROWS, ROWS), F32),
            vmem(part, F32),
            vmem((4,) + part, F32),
            vmem((8,) + part, F32),
            vmem((8,) + part, F32),
            vmem((2,) + part, F32),
            dma((7,)),
            dma((2,)),
            dma((2,)),
            dma((2, 4, STEPS)),
            dma((2, 4, STEPS)),
            dma((2, 2, STEPS)),
            dma((2, 2, STEPS)),
            dma((2,)),
            dma((2, 4)),
            dma((2, 8)),
            dma((2, 8)),
            dma((2,)),
        ],
        compiler_params=pltpu.CompilerParams(
            collective_id=0, has_side_effects=True, vmem_limit_bytes=56 * 1024 * 1024
        ),
        cost_estimate=pl.CostEstimate(
            flops=HEADS * 8 * 256 * 256 * 128, bytes_accessed=5 << 20, transcendentals=HEADS * 256 * 256
        ),
    )(q_pre[0], k_pre[0], values[0], grad_out[0], segment_ids, gain_q, gain_k)
    return out_q[None], out_k[None], sums[0], sums[1]


def solution(mesh):
    tokens = P("dp", "fsdp", None)
    return jax.shard_map(
        per_device,
        mesh=mesh,
        in_specs=(tokens, tokens, tokens, tokens, P("dp", "fsdp"), P(), P()),
        out_specs=(tokens, tokens, P(), P()),
        check_vma=False,
    )
```

time: 347 us -> 67.5 us (0.19); the launches traced: 342 us -> 67.2 us
  matrix products: 134 us -> 0 us
  blocking collectives: 108 us -> 0 us
  Pallas kernels: 0 us -> 62.2 us
  waiting for transfers between devices: 33.9 us -> 0 us
  other arithmetic: 27.7 us -> 0 us
  starting transfers between devices: 20.6 us -> 0 us
  local copies, waits for them, and re-layouts: 16.3 us -> 4.35 us
    dot_general x96 -> x0, matrix products: 134 us -> none  [the longest x24 40.6 us: one_head(): dk_head = jnp.dot(slopes.T, q_head, preferred_element_type=jnp.float32)]
    psum x1 -> x0, blocking collectives: 108 us -> none  [per_device(): total_q, total_k = lax.psum((dgain_q, dgain_k), ('dp', 'fsdp'))]
    pallas_call x0 -> x1, Pallas kernels: none -> 62.2 us  [per_device(): pl.pallas_call(kernel, out_shape=[jax.ShapeDtypeStruct(wide, BF16), jax.S...]
    ppermute x5 -> x0, waiting for transfers between devices: 33.9 us -> none  [from_behind(): return lax.ppermute(block, axis, route)]
    ppermute x5 -> x0, starting transfers between devices: 20.6 us -> none  [from_behind(): return lax.ppermute(block, axis, route)]
    convert_element_type x28 -> x0, other arithmetic: 9.56 us -> none  [the longest x24 3.04 us: one_head(): slopes = (probs * (dprob - delta) * scale).astype(jnp.bfloat16)]
    reduce_sum x30 -> x0, other arithmetic: 8.77 us -> none  [the longest x2 5.13 us: layer_norm(): return centered * lax.rsqrt(var + 1e-06) * gain]
    unnamed x44 -> x4, local copies, waits for them, and re-layouts: 9.73 us -> 3.02 us
  transfers between devices with their start and end apart: 5 -> 0, of which waited for: 3 -> 0; matrix products, arithmetic and copies ran while one was open for 2% -> 0% of each run, Pallas kernels for 0% -> 0%
where the time goes in v1:
time: 67.5 us; the launch traced here: 67.2 us
  Pallas kernels  62.2 us (92%)
  local copies, waits for them, and re-layouts  4.35 us (6%)
    pallas_call x1, Pallas kernels, per_device(): pl.pallas_call(kernel, out_shape=[jax.ShapeDtypeStruct(wide, BF16), jax.S...  62.2 us
    unnamed x4, local copies, waits for them, and re-layouts  3.02 us

profile of v1, /device:TPU:1, one launch (start us, length us, event | category | flops | bytes accessed | tf_op | source)
XLA Modules:
  0.0 67.2 jit_solution(9244623126699894478)
XLA Ops:
  0.6 62.2 %shard_map.102 = (bf16[128,3072]{1,0:T(8,128)(2,1)}, bf16[128,3072]{1,0:T(8,128)(2,1)}, f32[2,24,128]{2,1,0:T(8,128)}) custom-call(bf16[128,3072]{1,0:T(8,128)(2,1)} %bitcast.12, bf16[128,3072]{1,0:T(8,128)(2,1)} %bitcast.13, bf16[128,3072]{1,0:T(8,128)(2,1)} %bitcast.14, bf16[128,3072]{1,0:T(8,128)(2,1)} %bitcast.15, s32[1,128]{1,0:T(1,128)} %ids_ref.1, ...), custom_call_target="tpu_custom_call" | custom-call | flops 1610612736 | bytes 5242880 | tf_op jit(solution)/shard_map/pallas_call | solution.py:292
  62.8 1.3 %slice_bitcast_fusion = (f32[24,128]{1,0:T(8,128)}, f32[24,128]{1,0:T(8,128)}) fusion(f32[2,24,128]{2,1,0:T(8,128)} %get-tuple-element.9), kind=kLoop, calls=%fused_computation | loop fusion | bytes 49152 | tf_op jit(solution)/shard_map/squeeze | solution.py:340
  64.2 0.0 copy-start
  64.2 2.1 %copy.13 = bf16[1,128,3072]{2,1,0:T(8,128)(2,1)} copy(bf16[1,128,3072]{2,1,0:T(8,128)(2,1)} %bitcast.11) | data formatting | bytes 1572864
  66.3 0.0 copy-done
  66.3 0.9 %copy.14 = bf16[1,128,3072]{2,1,0:T(8,128)(2,1)} copy(bf16[1,128,3072]{2,1,0:T(8,128)(2,1)S(1)} %bitcast.10) | data formatting | bytes 1572864
Async XLA Ops:
  64.2 2.1 %copy-start = (bf16[128,3072]{1,0:T(8,128)(2,1)S(1)}, bf16[128,3072]{1,0:T(8,128)(2,1)}, u32[]{:S(2)}) copy-start(bf16[128,3072]{1,0:T(8,128)(2,1)} %get-tuple-element.8) | copy-start | bytes 2359300

commit v2 on v1

--- a/solution.py
+++ b/solution.py
@@ -71,33 +71,32 @@
     }
 
 
-def greet(left, right):
-    barrier = pltpu.get_barrier_semaphore()
-    for device in (left, right):
-        pl.semaphore_signal(barrier, inc=1, device_id=device, device_id_type=MESH)
-    count = 2
-    for size, me, member in groups().values():
-        for i in range(1, size):
-            peer = member(lax.rem(me + i, size))
-            pl.semaphore_signal(barrier, inc=1, device_id=peer, device_id_type=MESH)
-        count += size - 1
-    return barrier, count
+def signal_around(sem, axes, distance):
+    for name in axes:
+        size, me, member = groups()[name]
+        for step in (distance, size - distance):
+            peer = member(lax.rem(me + step, size))
+            pl.semaphore_signal(sem, inc=1, device_id=peer, device_id_type=MESH)
+    return 2 * len(axes)
 
 
 def kernel(
     q_ref, k_ref, v_ref, g_ref, ids_ref, gain_q_ref, gain_k_ref,
-    out_q_ref, out_k_ref, sum_ref,
-    own, halo, sent_back, came_back, result, gains, d_gains,
+    result, sum_ref,
+    own, halo, sent_back, came_back, gains, d_gains,
     ids_in, ids_own, ids_near, bias, weight, given,
     core_in, x_in, y_in, z_in, final,
     local_sem, id_send, id_recv, far_send, far_recv, back_send, back_recv,
-    core_sem, x_sem, y_sem, z_sem, last_sem,
+    core_sem, x_sem, y_sem, z_sem, last_sem, heard_1, heard_2,
 ):
     f = lax.axis_index("fsdp")
     size = lax.axis_size("fsdp")
     left = {"fsdp": lax.rem(f + size - 1, size)}
     right = {"fsdp": lax.rem(f + 1, size)}
-    barrier, count = greet(left, right)
+    barrier = pltpu.get_barrier_semaphore()
+    for device in (left, right):
+        pl.semaphore_signal(barrier, inc=1, device_id=device, device_id_type=MESH)
+    count = 2 + signal_around(barrier, "xyz", 1)
 
     sources = (q_ref, k_ref, v_ref, g_ref)
     loads = [pltpu.make_async_copy(ids_ref, ids_in, local_sem.at[4])]
@@ -146,6 +145,7 @@
         return carry
 
     lax.fori_loop(0, STEPS, send_far, 0)
+    near = signal_around(heard_1, "xyz", 1)
 
     for side in (0, 1):
         id_copy(side).wait()
@@ -177,6 +177,8 @@
     weight[...] = jnp.broadcast_to(weight_row, (ROWS, 2 * ROWS)).T
     given[...] = jnp.broadcast_to(given_row, (ROWS, ROWS)).T
 
+    pl.semaphore_wait(heard_1, near)
+    next_near = signal_around(heard_2, "yz", 2)
     for load in loads[1:]:
         load.wait()
 
@@ -196,18 +198,14 @@
                 d_raw = normalize_back(grads[i], unit[i], inverse[i], gain[i])
                 result[i, :, columns] = d_raw[:ROWS]
                 sent_back[i, :, columns] = d_raw[ROWS:]
-        return carry
-
-    lax.fori_loop(0, STEPS, compute, 0)
-
-    def send_back(step, carry):
         for array in range(2):
             for side in (0, 1):
                 back_copy(step, array, side).start()
         return carry
 
-    lax.fori_loop(0, STEPS, send_back, 0)
-
+    lax.fori_loop(0, STEPS, compute, 0)
+
+    pl.semaphore_wait(heard_2, next_near)
     members = groups()
     core = members["core"][1]
     other = 1 - core
@@ -260,11 +258,6 @@
         return carry
 
     lax.fori_loop(0, STEPS, finish, 0)
-    stores = [
-        pltpu.make_async_copy(result.at[i], out, local_sem.at[i]) for i, out in enumerate((out_q_ref, out_k_ref))
-    ]
-    for store in stores:
-        store.start()
     final[core] = total(z_in, copies)
     last_copy = core_copy(final.at[core], final.at[core], last_sem)
     last_copy.start()
@@ -280,8 +273,15 @@
         return carry
 
     lax.fori_loop(0, STEPS, drain, 0)
-    for store in stores:
-        store.wait()
+
+
+def hand_out(result, sums, out_q, out_k, sum_q, sum_k, sem):
+    copies = [pltpu.make_async_copy(result.at[i], out, sem.at[i]) for i, out in enumerate((out_q, out_k))]
+    copies += [pltpu.make_async_copy(sums.at[i], out, sem.at[2 + i]) for i, out in enumerate((sum_q, sum_k))]
+    for copy in copies:
+        copy.start()
+    for copy in copies:
+        copy.wait()
 
 
 def per_device(q_pre, k_pre, values, grad_out, segment_ids, gain_q, gain_k):
@@ -289,19 +289,14 @@
     vmem, dma = pltpu.VMEM, pltpu.SemaphoreType.DMA
     wide = (ROWS, WIDTH)
     part = (HEADS, DEPTH)
-    out_q, out_k, sums = pl.pallas_call(
+    result, sums = pl.pallas_call(
         kernel,
-        out_shape=[
-            jax.ShapeDtypeStruct(wide, BF16),
-            jax.ShapeDtypeStruct(wide, BF16),
-            jax.ShapeDtypeStruct((2,) + part, F32),
-        ],
+        out_shape=[vmem((2,) + wide, BF16), vmem((2,) + part, F32)],
         in_specs=[anywhere] * 7,
-        out_specs=[anywhere, anywhere, pl.BlockSpec(memory_space=vmem)],
+        out_specs=[pl.BlockSpec(memory_space=vmem)] * 2,
         scratch_shapes=[
             vmem((4,) + wide, BF16),
             vmem((4,) + wide, BF16),
-            vmem((2,) + wide, BF16),
             vmem((2,) + wide, BF16),
             vmem((2,) + wide, BF16),
             vmem((2,) + part, F32),
@@ -329,6 +324,8 @@
             dma((2, 8)),
             dma((2, 8)),
             dma((2,)),
+            pltpu.SemaphoreType.REGULAR,
+            pltpu.SemaphoreType.REGULAR,
         ],
         compiler_params=pltpu.CompilerParams(
             collective_id=0, has_side_effects=True, vmem_limit_bytes=56 * 1024 * 1024
@@ -337,7 +334,19 @@
             flops=HEADS * 8 * 256 * 256 * 128, bytes_accessed=5 << 20, transcendentals=HEADS * 256 * 256
         ),
     )(q_pre[0], k_pre[0], values[0], grad_out[0], segment_ids, gain_q, gain_k)
-    return out_q[None], out_k[None], sums[0], sums[1]
+    out_q, out_k, sum_q, sum_k = pl.pallas_call(
+        hand_out,
+        out_shape=[
+            jax.ShapeDtypeStruct(wide, BF16),
+            jax.ShapeDtypeStruct(wide, BF16),
+            jax.ShapeDtypeStruct(part, F32),
+            jax.ShapeDtypeStruct(part, F32),
+        ],
+        in_specs=[pl.BlockSpec(memory_space=vmem)] * 2,
+        out_specs=[anywhere] * 4,
+        scratch_shapes=[dma((4,))],
+    )(result, sums)
+    return out_q[None], out_k[None], sum_q, sum_k
 
 
 def solution(mesh):

time: 67.5 us -> 62.7 us (0.929)
  local copies, waits for them, and re-layouts: 4.35 us -> 1.76 us
  Pallas kernels: 62.2 us -> 60.2 us
    pallas_call x1 -> x2, Pallas kernels: 62.2 us -> 60.2 us  [the longest x1 57.6 us: per_device(): pl.pallas_call(kernel, out_shape=[vmem((2,) + wide, BF16), vmem((2,) + pa...]
    squeeze x1 -> x0, local copies, waits for them, and re-layouts: 1.33 us -> none  [per_device(): return (out_q[None], out_k[None], sums[0], sums[1])]
    unnamed x4, local copies, waits for them, and re-layouts: 3.02 us -> 1.76 us
where the time goes in v2:
time: 62.7 us; the launch traced here: 62.6 us
  Pallas kernels  60.2 us (96%)
  local copies, waits for them, and re-layouts  1.76 us (3%)
  between operations  0.65 us (1%)
    pallas_call x1, Pallas kernels, per_device(): pl.pallas_call(kernel, out_shape=[vmem((2,) + wide, BF16), vmem((2,) + pa...  57.6 us
    pallas_call x1, Pallas kernels, per_device(): pl.pallas_call(hand_out, out_shape=[jax.ShapeDtypeStruct(wide, BF16), jax...  2.58 us
    unnamed x4, local copies, waits for them, and re-layouts  1.76 us

profile of v2, /device:TPU:1, one launch (start us, length us, event | category | flops | bytes accessed | tf_op | source)
XLA Modules:
  0.0 62.6 jit_solution(563028881352818002)
XLA Ops:
  0.6 57.6 %shard_map.102 = (bf16[2,128,3072]{2,1,0:T(8,128)(2,1)S(1)}, f32[2,24,128]{2,1,0:T(8,128)S(1)}) custom-call(bf16[128,3072]{1,0:T(8,128)(2,1)} %bitcast.6, bf16[128,3072]{1,0:T(8,128)(2,1)} %bitcast.7, bf16[128,3072]{1,0:T(8,128)(2,1)} %bitcast.8, bf16[128,3072]{1,0:T(8,128)(2,1)} %bitcast.9, s32[1,128]{1,0:T(1,128)} %ids_ref.1, f32[24,128]{1,0:T(8,128)} %gain_q_ref.1, ...), custom_call_target="tpu_custom_call" | custom-call | flops 1610612736 | bytes 5242880 | tf_op jit(solution)/shard_map/pallas_call | solution.py:292
  58.2 0.0 copy-start
  58.2 1.2 %copy-done = bf16[2,128,3072]{2,1,0:T(8,128)(2,1)} copy-done((bf16[2,128,3072]{2,1,0:T(8,128)(2,1)}, bf16[2,128,3072]{2,1,0:T(8,128)(2,1)S(1)}, u32[]{:S(2)}) %copy-start) | copy-done | bytes 1572888
  59.4 0.0 copy-start.1
  59.4 0.6 copy-done.1
  60.0 2.6 %shard_map.103 = (bf16[128,3072]{1,0:T(8,128)(2,1)}, bf16[128,3072]{1,0:T(8,128)(2,1)}, f32[24,128]{1,0:T(8,128)}, f32[24,128]{1,0:T(8,128)}) custom-call(bf16[2,128,3072]{2,1,0:T(8,128)(2,1)} %copy-done, f32[2,24,128]{2,1,0:T(8,128)} %copy-done.1), custom_call_target="tpu_custom_call" | custom-call | tf_op jit(solution)/shard_map/pallas_call | solution.py:337
Async XLA Ops:
  58.2 1.2 %copy-start = (bf16[2,128,3072]{2,1,0:T(8,128)(2,1)}, bf16[2,128,3072]{2,1,0:T(8,128)(2,1)S(1)}, u32[]{:S(2)}) copy-start(bf16[2,128,3072]{2,1,0:T(8,128)(2,1)S(1)} %get-tuple-element.10.result) | copy-start | bytes 4718596
  59.4 0.6 copy-start.1

commit v3 on v2

--- a/solution.py
+++ b/solution.py
@@ -85,9 +85,9 @@
     result, sum_ref,
     own, halo, sent_back, came_back, gains, d_gains,
     ids_in, ids_own, ids_near, bias, weight, given,
-    core_in, x_in, y_in, z_in, final,
+    core_in, x_in, y_in, z_in,
     local_sem, id_send, id_recv, far_send, far_recv, back_send, back_recv,
-    core_sem, x_sem, y_sem, z_sem, last_sem, heard_1, heard_2,
+    core_sem, x_sem, y_sem, z_sem, heard_1, heard_2,
 ):
     f = lax.axis_index("fsdp")
     size = lax.axis_size("fsdp")
@@ -208,21 +208,16 @@
     pl.semaphore_wait(heard_2, next_near)
     members = groups()
     core = members["core"][1]
-    other = 1 - core
-
-    def core_copy(source, target, pair):
-        return pltpu.make_async_remote_copy(
-            src_ref=source, dst_ref=target, send_sem=pair.at[0], recv_sem=pair.at[1],
-            device_id=members["core"][2](other), device_id_type=MESH,
-        )
-
-    first_copy = core_copy(d_gains.at[other], core_in, core_sem)
-    first_copy.start()
-    first_copy.wait()
+    swap = pltpu.make_async_remote_copy(
+        src_ref=d_gains, dst_ref=core_in, send_sem=core_sem.at[0], recv_sem=core_sem.at[1],
+        device_id=members["core"][2](1 - core), device_id_type=MESH,
+    )
+    swap.start()
+    swap.wait()
 
     def exchange(name, block, slots, sems):
         size, me, member = members[name]
-        slots[me] = block
+        slots[me] = block.astype(BF16)
         copies = []
         for i in range(1, size):
             peer = lax.rem(me + i, size)
@@ -239,9 +234,9 @@
     def total(slots, copies):
         for copy in copies:
             copy.wait()
-        return jnp.sum(slots[...], 0)
-
-    copies = exchange("x", d_gains[core] + core_in[...], x_in, x_sem)
+        return jnp.sum(slots[...].astype(F32), 0)
+
+    copies = exchange("x", d_gains[...].reshape(2 * HEADS, DEPTH) + core_in[...].reshape(2 * HEADS, DEPTH), x_in, x_sem)
     copies = exchange("y", total(x_in, copies), y_in, y_sem)
     copies = exchange("z", total(y_in, copies), z_in, z_sem)
 
@@ -258,11 +253,7 @@
         return carry
 
     lax.fori_loop(0, STEPS, finish, 0)
-    final[core] = total(z_in, copies)
-    last_copy = core_copy(final.at[core], final.at[core], last_sem)
-    last_copy.start()
-    last_copy.wait()
-    sum_ref[...] = final[...]
+    sum_ref[...] = total(z_in, copies).reshape(2, HEADS, DEPTH)
 
     def drain(step, carry):
         for side in (0, 1):
@@ -307,11 +298,10 @@
             vmem((2 * ROWS, 2 * ROWS), F32),
             vmem((2 * ROWS, ROWS), F32),
             vmem((ROWS, ROWS), F32),
-            vmem(part, F32),
-            vmem((4,) + part, F32),
-            vmem((8,) + part, F32),
-            vmem((8,) + part, F32),
             vmem((2,) + part, F32),
+            vmem((4, 2 * HEADS, DEPTH), BF16),
+            vmem((8, 2 * HEADS, DEPTH), BF16),
+            vmem((8, 2 * HEADS, DEPTH), BF16),
             dma((7,)),
             dma((2,)),
             dma((2,)),
@@ -323,7 +313,6 @@
             dma((2, 4)),
             dma((2, 8)),
             dma((2, 8)),
-            dma((2,)),
             pltpu.SemaphoreType.REGULAR,
             pltpu.SemaphoreType.REGULAR,
         ],
@@ -345,6 +334,7 @@
         in_specs=[pl.BlockSpec(memory_space=vmem)] * 2,
         out_specs=[anywhere] * 4,
         scratch_shapes=[dma((4,))],
+        compiler_params=pltpu.CompilerParams(vmem_limit_bytes=4 * 1024 * 1024),
     )(result, sums)
     return out_q[None], out_k[None], sum_q, sum_k
 

time: 62.7 us -> 57.9 us (0.923)
  the two profiles are of different devices: /device:TPU:1 before, /device:TPU:6 now
where the time goes in v3:
time: 57.9 us; the launch traced here: 57.8 us
  Pallas kernels  57.2 us (99%)
  between operations  0.64 us (1%)
    pallas_call x1, Pallas kernels, per_device(): pl.pallas_call(kernel, out_shape=[vmem((2,) + wide, BF16), vmem((2,) + pa...  56 us
    pallas_call x1, Pallas kernels, per_device(): pl.pallas_call(hand_out, out_shape=[jax.ShapeDtypeStruct(wide, BF16), jax...  1.18 us

profile of v3, /device:TPU:6, one launch (start us, length us, event | category | flops | bytes accessed | tf_op | source)
XLA Modules:
  0.0 57.8 jit_solution(2066505690063719222)
XLA Ops:
  0.6 56.0 %shard_map.102 = (bf16[2,128,3072]{2,1,0:T(8,128)(2,1)S(1)}, f32[2,24,128]{2,1,0:T(8,128)S(1)}) custom-call(bf16[128,3072]{1,0:T(8,128)(2,1)} %bitcast.6, bf16[128,3072]{1,0:T(8,128)(2,1)} %bitcast.7, bf16[128,3072]{1,0:T(8,128)(2,1)} %bitcast.8, bf16[128,3072]{1,0:T(8,128)(2,1)} %bitcast.9, s32[1,128]{1,0:T(1,128)} %ids_ref.1, f32[24,128]{1,0:T(8,128)} %gain_q_ref.1, ...), custom_call_target="tpu_custom_call" | custom-call | flops 1610612736 | bytes 5242880 | tf_op jit(solution)/shard_map/pallas_call | solution.py:283
  56.6 1.2 %shard_map.103 = (bf16[128,3072]{1,0:T(8,128)(2,1)}, bf16[128,3072]{1,0:T(8,128)(2,1)}, f32[24,128]{1,0:T(8,128)}, f32[24,128]{1,0:T(8,128)}) custom-call(bf16[2,128,3072]{2,1,0:T(8,128)(2,1)S(1)} %get-tuple-element.10.result, f32[2,24,128]{2,1,0:T(8,128)S(1)} %get-tuple-element.11.sums), custom_call_target="tpu_custom_call" | custom-call | tf_op jit(solution)/shard_map/pallas_call | solution.py:326

commit v4 on v3

v4 whole, which is shorter than its diff:
```python
import math

import jax
import jax.numpy as jnp
from jax import lax
from jax.experimental import pallas as pl
from jax.experimental.pallas import tpu as pltpu
from jax.sharding import PartitionSpec as P

MESH = pl.DeviceIdType.MESH
F32 = jnp.float32
BF16 = jnp.bfloat16

HEADS = 24
DEPTH = 128
ROWS = 128
WIDTH = HEADS * DEPTH
NEAR_HEADS = HEADS // 2
NEAR_WIDTH = NEAR_HEADS * DEPTH
AT_ONCE = 4
TILE = 16
TILES = ROWS // TILE
SLOTS = 56
PIECES = (0, 32, 40, 48, 56)
MOST = (20, 19, 16, 13, 11, 8, 5, 4)
PLACES = ((0, 1, 2, 3), (16, 17, 18, 19), (4, 5, 6, 7), (8, 9, 10, 11), (12, 13, 14, 15))
SCALE = DEPTH**-0.5
SCALE_LOG2 = SCALE * math.log2(math.e)


def dot(a, b, contract_a, contract_b):
    dims = (((contract_a,), (contract_b,)), ((), ()))
    return lax.dot_general(a, b, dims, preferred_element_type=F32)


def lane_mean(x):
    return jnp.sum(x, -1, keepdims=True) * (1.0 / DEPTH)


def normalize(x, gain):
    centered = x - lane_mean(x)
    inverse = lax.rsqrt(lane_mean(centered * centered) + 1e-06)
    unit = centered * inverse
    return unit, inverse, (unit * gain).astype(BF16)


def normalize_back(grad, unit, inverse, gain):
    d_unit = grad * gain
    mean = lane_mean(d_unit)
    slope = lane_mean(d_unit * unit)
    return (inverse * (d_unit - mean - unit * slope)).astype(BF16)


def diagonal(pair):
    zero = jnp.zeros((DEPTH, DEPTH), BF16)
    return jnp.concatenate(
        [jnp.concatenate([pair[0], zero], 1), jnp.concatenate([zero, pair[1]], 1)], 0
    )


def attention_back(queries, keys, values, cotangent, bias):
    both_keys = jnp.concatenate(keys, 1)
    both_queries = diagonal(queries)
    scores = dot(both_keys, both_queries, 1, 1) * SCALE_LOG2 + jnp.concatenate([bias, bias], 1)
    expo = jnp.exp2(scores - jnp.max(scores, 0, keepdims=True))
    total = jnp.sum(expo, 0, keepdims=True)
    dprob = dot(jnp.concatenate(values, 1), diagonal(cotangent), 1, 1)
    delta = jnp.sum(expo * dprob, 0, keepdims=True) / total
    slopes = (expo * (SCALE / total) * (dprob - delta)).astype(BF16)
    dq = dot(slopes, both_keys, 0, 0)
    dk = dot(slopes, both_queries, 1, 0)
    return [dq[:ROWS, :DEPTH], dq[ROWS:, DEPTH:]], [dk[:, :DEPTH], dk[:, DEPTH:]]


def place():
    f = lax.axis_index("fsdp")
    return lax.axis_index("dp"), f // 16, lax.rem(f, 16) // 2, lax.rem(f, 2)


def groups():
    y, x, z, c = place()
    return {
        "core": (2, c, lambda j: {"fsdp": x * 16 + z * 2 + j}),
        "x": (4, x, lambda j: {"fsdp": j * 16 + z * 2 + c}),
        "y": (8, y, lambda j: {"dp": j}),
        "z": (8, z, lambda j: {"fsdp": x * 16 + j * 2 + c}),
    }


def signal_around(sem, axes, distance):
    for name in axes:
        size, me, member = groups()[name]
        for step in (distance, size - distance):
            peer = member(lax.rem(me + step, size))
            pl.semaphore_signal(sem, inc=1, device_id=peer, device_id_type=MESH)
    return 2 * len(axes)


def kernel(
    q_ref, k_ref, v_ref, g_ref, ids_ref, gain_q_ref, gain_k_ref,
    result, sum_ref,
    own, near_in, near_out, near_back, packed, arrived,
    far_out, back_packed, back_tiles, gains, d_gains,
    ids_in, ids_own, ids_next, bias, weight, masks, own_terms, counts, cases, window,
    core_in, x_in, y_in, z_in,
    local_sem, near_id_sem, far_id_sem, near_sem, far_sem, near_back_sem, far_back_sem,
    core_sem, x_sem, y_sem, z_sem, heard_1, heard_2,
):
    f = lax.axis_index("fsdp")
    size = lax.axis_size("fsdp")
    core = lax.rem(f, 2)
    left, right = lax.rem(f + size - 1, size), lax.rem(f + 1, size)
    near = {"fsdp": f + 1 - 2 * core}
    far = {"fsdp": lax.rem(f + size - 1 + 2 * core, size)}
    barrier = pltpu.get_barrier_semaphore()
    for device in (left, right):
        pl.semaphore_signal(barrier, inc=1, device_id={"fsdp": device}, device_id_type=MESH)
    count = 2 + signal_around(barrier, "xyz", 1)

    sources = (q_ref, k_ref, v_ref, g_ref)
    loads = [pltpu.make_async_copy(ids_ref, ids_in, local_sem.at[4])]
    loads += [pltpu.make_async_copy(s, own.at[i], local_sem.at[i]) for i, s in enumerate(sources)]
    loads += [
        pltpu.make_async_copy(gain_q_ref, gains.at[0], local_sem.at[5]),
        pltpu.make_async_copy(gain_k_ref, gains.at[1], local_sem.at[6]),
    ]
    for load in loads:
        load.start()
    loads[0].wait()
    ids_own[...] = jnp.broadcast_to(ids_in[...], (8, ROWS))

    def remote(source, target, pair, device):
        return pltpu.make_async_remote_copy(
            src_ref=source, dst_ref=target, send_sem=pair.at[0], recv_sem=pair.at[1],
            device_id=device, device_id_type=MESH,
        )

    mine = ids_own[0:1, :]
    lane = lax.broadcasted_iota(jnp.int32, (1, ROWS), 1)

    def down(row):
        return jnp.broadcast_to(row, (ROWS, ROWS)).T

    def set_bias(place, row):
        across = jnp.broadcast_to(row, (ROWS, ROWS))
        bias[place] = jnp.where(across == across.T, 0.0, -1e30).astype(F32)

    def head_columns(head):
        return pl.ds(pl.multiple_of(head * DEPTH, DEPTH), DEPTH)

    def image_back(raw, heads, place):
        gain = [[gains[i, pl.ds(head, 1), :] for head in heads] for i in range(2)]
        normed = [[normalize(raw[i][h].astype(F32), gain[i][h]) for h in range(2)] for i in range(2)]
        halves = [[normed[i][h][2] for h in range(2)] for i in range(2)]
        grads = attention_back(halves[0], halves[1], raw[2], raw[3], bias[place])
        terms = [[grads[i][h] * normed[i][h][0] for h in range(2)] for i in range(2)]
        d_raw = [
            [normalize_back(grads[i][h], normed[i][h][0], normed[i][h][1], gain[i][h]) for h in range(2)]
            for i in range(2)
        ]
        return d_raw, terms

    def weigh(term, place):
        return jnp.sum(term * weight[place], 0, keepdims=True)

    def alone(step, carry):
        for part in range(AT_ONCE // 2):
            heads = [step * AT_ONCE + part * 2 + h for h in range(2)]
            columns = [head_columns(head) for head in heads]
            d_raw, terms = image_back([[own[i, :, c] for c in columns] for i in range(4)], heads, 0)
            for i in range(2):
                for h in range(2):
                    result[i, :, columns[h]] = d_raw[i][h]
                    own_terms[heads[h], i] = terms[i][h]
        return carry

    def sum_alone(head, carry):
        for i in range(2):
            d_gains[i, pl.ds(head, 1), :] = weigh(own_terms[head, i], 0)
        return carry

    set_bias(0, mine.astype(F32))
    for load in loads[1:]:
        load.wait()
    lax.fori_loop(0, 2, alone, 0)
    pl.semaphore_wait(barrier, count)

    id_copies = [
        remote(ids_own, ids_next.at[i], sems, device)
        for i, sems, device in ((0, near_id_sem, near), (1, far_id_sem, far))
    ]
    for copy in id_copies:
        copy.start()
    away = pl.ds(pl.multiple_of((1 - core) * NEAR_WIDTH, DEPTH), NEAR_WIDTH)
    near_copies = [remote(own.at[i, :, away], near_in.at[i], near_sem.at[i], near) for i in range(4)]
    for copy in near_copies:
        copy.start()
    heard = signal_around(heard_1, "xyz", 1)

    lax.fori_loop(2, 4, alone, 0)
    for copy in id_copies:
        copy.wait()
    pl.semaphore_wait(heard_1, heard)
    next_heard = signal_around(heard_2, "yz", 2)

    def pick(x, at):
        return jnp.sum(jnp.where(lane == at, x, 0), -1, keepdims=True)

    def shared(other, at_end):
        my_edge = jnp.where(at_end, ROWS - 1, 0)
        own_rows = mine == pick(other, ROWS - 1 - my_edge)
        other_rows = other == pick(mine, my_edge)
        return own_rows, other_rows

    follows = core == 1
    has_far = jnp.where(follows, f < size - 1, f > 0)
    far_ids = jnp.where(has_far, ids_next[1, 0:1, :], -2)
    near_own, near_other = shared(ids_next[0, 0:1, :], core == 0)
    far_own, far_other = shared(far_ids, follows)
    near_used, far_used = near_own | near_other, far_own | far_other
    set_bias(1, near_used.astype(F32))
    set_bias(2, far_used.astype(F32))
    weight[0] = down(1.0 - (near_own | far_own).astype(F32))
    weight[1] = down(near_used.astype(F32))
    weight[2] = down(far_used.astype(F32))
    for i, row in enumerate((near_own, near_other, far_own, far_other)):
        masks[i] = down(row.astype(F32)).astype(BF16)

    def tiles_of(rows):
        return (jnp.sum(rows.astype(jnp.int32), -1, keepdims=True) + (TILE - 1)) >> 4

    my_tiles, other_tiles = tiles_of(far_own), tiles_of(far_other)
    begin_tiles = jnp.where(follows, my_tiles, other_tiles)
    split = jnp.full((1, 1), 4, jnp.int32)
    for least, more in ((2, 1), (3, 3), (4, 3), (5, 2), (6, 3), (7, 3), (8, 1)):
        split = split + jnp.where(begin_tiles >= least, more, 0)
    rest = HEADS - split
    counts[0:1, :] = jnp.broadcast_to(jnp.where(follows, split, rest), (1, DEPTH))
    counts[1:2, :] = jnp.broadcast_to(jnp.where(follows, rest, split), (1, DEPTH))
    for case in range(TILES):
        for i, tiles in enumerate((my_tiles, other_tiles)):
            cases[i, case] = jnp.broadcast_to((tiles == case + 1).astype(F32), (TILE, DEPTH)).astype(BF16)

    kept_heads = [core * p + (1 - core) * (HEADS - 1 - p) for p in range(MOST[0])]
    sent_heads = [core * (HEADS - 1 - p) + (1 - core) * p for p in range(MOST[0])]
    my_rows = [(core * (TILES - 1 - u) + (1 - core) * u) * TILE for u in range(TILES)]
    other_rows_at = [(core * u + (1 - core) * (TILES - 1 - u)) * TILE for u in range(TILES)]

    def tile_rows(starts, u):
        return pl.ds(pl.multiple_of(starts[u], TILE), TILE)

    def chosen(side, terms):
        block = None
        for case, value in terms:
            term = value * cases[side, case]
            block = term if block is None else block + term
        return jnp.zeros((TILE, DEPTH), BF16) if block is None else block

    def cases_of_slot(slot):
        return [(n - 1, slot // n, slot % n) for n in range(1, TILES + 1) if slot < MOST[n - 1] * n]

    def cases_of_tile(place, u):
        return [(n - 1, place * n + u) for n in range(u + 1, TILES + 1) if place < MOST[n - 1]]

    far_copies = []
    for piece in range(len(PIECES) - 1):
        for slot in range(PIECES[piece], PIECES[piece + 1]):
            for i in range(4):
                packed[slot, i] = chosen(
                    0,
                    [
                        (case, own[i, tile_rows(my_rows, u), head_columns(sent_heads[place])])
                        for case, place, u in cases_of_slot(slot)
                    ],
                )
        span = pl.ds(PIECES[piece], PIECES[piece + 1] - PIECES[piece])
        copy = remote(packed.at[span], arrived.at[span], far_sem.at[piece], far)
        copy.start()
        far_copies.append(copy)

    lax.fori_loop(4, HEADS // AT_ONCE, alone, 0)
    lax.fori_loop(0, HEADS, sum_alone, 0, unroll=2)

    def between_cores(step, carry):
        own_rows, other_rows = masks[0] != 0, masks[1] != 0
        for part in range(AT_ONCE // 2):
            places = [step * AT_ONCE + part * 2 + h for h in range(2)]
            heads = [core * NEAR_HEADS + place for place in places]
            columns, inner = [head_columns(h) for h in heads], [head_columns(p) for p in places]
            raw = [
                [jnp.where(other_rows, near_in[i, :, inner[h]], own[i, :, columns[h]]) for h in range(2)]
                for i in range(4)
            ]
            d_raw, terms = image_back(raw, heads, 1)
            for i in range(2):
                for h in range(2):
                    result[i, :, columns[h]] = jnp.where(own_rows, d_raw[i][h], result[i, :, columns[h]])
                    near_out[i, :, inner[h]] = d_raw[i][h]
                    d_gains[i, pl.ds(heads[h], 1), :] += weigh(terms[i][h], 1)
        return carry

    for copy in near_copies:
        copy.wait_recv()
    lax.fori_loop(0, NEAR_HEADS // AT_ONCE, between_cores, 0)
    near_return = remote(near_out, near_back, near_back_sem, near)
    near_return.start()

    def between_chips(places):
        other_rows = masks[3] != 0
        for h, place in enumerate(places):
            for u in range(TILES):
                for i in range(4):
                    window[h, i, tile_rows(other_rows_at, u), :] = chosen(
                        1, [(case, arrived[slot, i]) for case, slot in cases_of_tile(place, u)]
                    )
        for first in range(0, len(places), 2):
            pair = places[first : first + 2]
            heads = [kept_heads[place] for place in pair]
            columns = [head_columns(head) for head in heads]
            here = [(counts[0:1, :] > place).astype(F32) for place in pair]
            raw = [
                [jnp.where(other_rows, window[first + h, i], own[i, :, columns[h]]) for h in range(2)]
                for i in range(4)
            ]
            d_raw, terms = image_back(raw, heads, 2)
            for h in range(2):
                changed = masks[2] * here[h].astype(BF16) != 0
                for i in range(2):
                    result[i, :, columns[h]] = jnp.where(changed, d_raw[i][h], result[i, :, columns[h]])
                    far_out[pair[h], i] = d_raw[i][h]
                    d_gains[i, pl.ds(heads[h], 1), :] += weigh(terms[i][h], 2) * here[h]

    waited = 0
    for places in PLACES:
        need = 1 + max(slot for p in places for u in range(TILES) for _, slot in cases_of_tile(p, u))
        while PIECES[waited] < need:
            far_copies[waited].wait_recv()
            waited += 1
        between_chips(places)

    pl.semaphore_wait(heard_2, next_heard)
    swap = remote(d_gains, core_in, core_sem, near)
    swap.start()

    members = groups()

    def exchange(name, block, slots, sems):
        size, me, member = members[name]
        slots[me] = block.astype(BF16)
        copies = []
        for i in range(1, size):
            peer = lax.rem(me + i, size)
            copies.append(
                pltpu.make_async_remote_copy(
                    src_ref=slots.at[me], dst_ref=slots.at[me], send_sem=sems.at[0, i], recv_sem=sems.at[1, size - i],
                    device_id=member(peer), device_id_type=MESH,
                )
            )
        for copy in copies:
            copy.start()
        return copies

    def total(slots, copies):
        for copy in copies:
            copy.wait()
        return jnp.sum(slots[...].astype(F32), 0)

    swap.wait()
    chip = d_gains[...].reshape(2 * HEADS, DEPTH) + core_in[...].reshape(2 * HEADS, DEPTH)
    copies = exchange("x", chip, x_in, x_sem)
    for slot in range(SLOTS):
        for i in range(2):
            back_packed[slot, i] = chosen(
                1,
                [
                    (case, far_out[place, i, tile_rows(other_rows_at, u), :])
                    for case, place, u in cases_of_slot(slot)
                ],
            )
    far_return = remote(back_packed, back_tiles, far_back_sem, far)
    far_return.start()
    copies = exchange("y", total(x_in, copies), y_in, y_sem)

    near_return.wait()

    def finish_near(place, carry):
        columns, inner = head_columns((1 - core) * NEAR_HEADS + place), head_columns(place)
        for i in range(2):
            result[i, :, columns] = jnp.where(masks[0] != 0, near_back[i, :, inner], result[i, :, columns])
        return carry

    lax.fori_loop(0, NEAR_HEADS, finish_near, 0)
    copies = exchange("z", total(y_in, copies), z_in, z_sem)
    far_return.wait()

    for place in range(MOST[0]):
        columns = head_columns(sent_heads[place])
        theirs = masks[2] * (counts[1:2, :] > place).astype(F32).astype(BF16) != 0
        for i in range(2):
            for u in range(TILES):
                window[place % 4, i, tile_rows(my_rows, u), :] = chosen(
                    0, [(case, back_tiles[slot, i]) for case, slot in cases_of_tile(place, u)]
                )
            result[i, :, columns] = jnp.where(theirs, window[place % 4, i], result[i, :, columns])
    sum_ref[...] = total(z_in, copies).reshape(2, HEADS, DEPTH)
    for copy in near_copies + far_copies:
        copy.wait_send()


def hand_out(result, sums, out_q, out_k, sum_q, sum_k, sem):
    copies = [pltpu.make_async_copy(result.at[i], out, sem.at[i]) for i, out in enumerate((out_q, out_k))]
    copies += [pltpu.make_async_copy(sums.at[i], out, sem.at[2 + i]) for i, out in enumerate((sum_q, sum_k))]
    for copy in copies:
        copy.start()
    for copy in copies:
        copy.wait()


def per_device(q_pre, k_pre, values, grad_out, segment_ids, gain_q, gain_k):
    anywhere = pl.BlockSpec(memory_space=pl.ANY)
    vmem, dma = pltpu.VMEM, pltpu.SemaphoreType.DMA
    wide = (ROWS, WIDTH)
    part = (HEADS, DEPTH)
    result, sums = pl.pallas_call(
        kernel,
        out_shape=[vmem((2,) + wide, BF16), vmem((2,) + part, F32)],
        in_specs=[anywhere] * 7,
        out_specs=[pl.BlockSpec(memory_space=vmem)] * 2,
        scratch_shapes=[
            vmem((4,) + wide, BF16),
            vmem((4, ROWS, NEAR_WIDTH), BF16),
            vmem((2, ROWS, NEAR_WIDTH), BF16),
            vmem((2, ROWS, NEAR_WIDTH), BF16),
            vmem((SLOTS, 4, TILE, DEPTH), BF16),
            vmem((SLOTS, 4, TILE, DEPTH), BF16),
            vmem((MOST[0], 2, ROWS, DEPTH), BF16),
            vmem((SLOTS, 2, TILE, DEPTH), BF16),
            vmem((SLOTS, 2, TILE, DEPTH), BF16),
            vmem((2,) + part, F32),
            vmem((2,) + part, F32),
            vmem((1, ROWS), jnp.int32),
            vmem((8, ROWS), jnp.int32),
            vmem((2, 8, ROWS), jnp.int32),
            vmem((3, ROWS, ROWS), F32),
            vmem((3, ROWS, ROWS), F32),
            vmem((4, ROWS, ROWS), BF16),
            vmem((HEADS, 2, ROWS, DEPTH), F32),
            vmem((8, DEPTH), jnp.int32),
            vmem((2, TILES, TILE, DEPTH), BF16),
            vmem((4, 4, ROWS, DEPTH), BF16),
            vmem((2,) + part, F32),
            vmem((4, 2 * HEADS, DEPTH), BF16),
            vmem((8, 2 * HEADS, DEPTH), BF16),
            vmem((8, 2 * HEADS, DEPTH), BF16),
            dma((7,)),
            dma((2,)),
            dma((2,)),
            dma((4, 2)),
            dma((len(PIECES) - 1, 2)),
            dma((2,)),
            dma((2,)),
            dma((2,)),
            dma((2, 4)),
            dma((2, 8)),
            dma((2, 8)),
            pltpu.SemaphoreType.REGULAR,
            pltpu.SemaphoreType.REGULAR,
        ],
        compiler_params=pltpu.CompilerParams(
            collective_id=0, has_side_effects=True, vmem_limit_bytes=56 * 1024 * 1024
        ),
        cost_estimate=pl.CostEstimate(
            flops=HEADS * 8 * 256 * 256 * 128, bytes_accessed=5 << 20, transcendentals=HEADS * 256 * 256
        ),
    )(q_pre[0], k_pre[0], values[0], grad_out[0], segment_ids, gain_q, gain_k)
    out_q, out_k, sum_q, sum_k = pl.pallas_call(
        hand_out,
        out_shape=[
            jax.ShapeDtypeStruct(wide, BF16),
            jax.ShapeDtypeStruct(wide, BF16),
            jax.ShapeDtypeStruct(part, F32),
            jax.ShapeDtypeStruct(part, F32),
        ],
        in_specs=[pl.BlockSpec(memory_space=vmem)] * 2,
        out_specs=[anywhere] * 4,
        scratch_shapes=[dma((4,))],
        compiler_params=pltpu.CompilerParams(vmem_limit_bytes=4 * 1024 * 1024),
    )(result, sums)
    return out_q[None], out_k[None], sum_q, sum_k


def solution(mesh):
    tokens = P("dp", "fsdp", None)
    return jax.shard_map(
        per_device,
        mesh=mesh,
        in_specs=(tokens, tokens, tokens, tokens, P("dp", "fsdp"), P(), P()),
        out_specs=(tokens, tokens, P(), P()),
        check_vma=False,
    )
```

time: 57.9 us -> 54.4 us (0.940)
  the two profiles are of different devices: /device:TPU:6 before, /device:TPU:2 now
where the time goes in v4:
time: 54.4 us; the launch traced here: 54.2 us
  Pallas kernels  53.4 us (98%)
  between operations  0.8 us (1%)
    pallas_call x1, Pallas kernels, per_device(): pl.pallas_call(kernel, out_shape=[vmem((2,) + wide, BF16), vmem((2,) + pa...  52.2 us
    pallas_call x1, Pallas kernels, per_device(): pl.pallas_call(hand_out, out_shape=[jax.ShapeDtypeStruct(wide, BF16), jax...  1.18 us

profile of v4, /device:TPU:2, one launch (start us, length us, event | category | flops | bytes accessed | tf_op | source)
XLA Modules:
  0.0 54.2 jit_solution(18098131642618180121)
XLA Ops:
  0.6 52.2 %shard_map.102 = (bf16[2,128,3072]{2,1,0:T(8,128)(2,1)S(1)}, f32[2,24,128]{2,1,0:T(8,128)S(1)}) custom-call(bf16[128,3072]{1,0:T(8,128)(2,1)} %bitcast.6, bf16[128,3072]{1,0:T(8,128)(2,1)} %bitcast.7, bf16[128,3072]{1,0:T(8,128)(2,1)} %bitcast.8, bf16[128,3072]{1,0:T(8,128)(2,1)} %bitcast.9, s32[1,128]{1,0:T(1,128)} %ids_ref.1, f32[24,128]{1,0:T(8,128)} %gain_q_ref.1, ...), custom_call_target="tpu_custom_call" | custom-call | flops 1610612736 | bytes 5242880 | tf_op jit(solution)/shard_map/pallas_call | solution.py:424
  52.9 1.2 %shard_map.103 = (bf16[128,3072]{1,0:T(8,128)(2,1)}, bf16[128,3072]{1,0:T(8,128)(2,1)}, f32[24,128]{1,0:T(8,128)}, f32[24,128]{1,0:T(8,128)}) custom-call(bf16[2,128,3072]{2,1,0:T(8,128)(2,1)S(1)} %get-tuple-element.10.result, f32[2,24,128]{2,1,0:T(8,128)S(1)} %get-tuple-element.11.sums), custom_call_target="tpu_custom_call" | custom-call | tf_op jit(solution)/shard_map/pallas_call | solution.py:476

commit v5 on v4

--- a/solution.py
+++ b/solution.py
@@ -17,7 +17,8 @@
 WIDTH = HEADS * DEPTH
 NEAR_HEADS = HEADS // 2
 NEAR_WIDTH = NEAR_HEADS * DEPTH
-AT_ONCE = 4
+ALONE_AT_ONCE = 8
+NEAR_AT_ONCE = 6
 TILE = 16
 TILES = ROWS // TILE
 SLOTS = 56
@@ -164,8 +165,8 @@
         return jnp.sum(term * weight[place], 0, keepdims=True)
 
     def alone(step, carry):
-        for part in range(AT_ONCE // 2):
-            heads = [step * AT_ONCE + part * 2 + h for h in range(2)]
+        for part in range(ALONE_AT_ONCE // 2):
+            heads = [step * ALONE_AT_ONCE + part * 2 + h for h in range(2)]
             columns = [head_columns(head) for head in heads]
             d_raw, terms = image_back([[own[i, :, c] for c in columns] for i in range(4)], heads, 0)
             for i in range(2):
@@ -182,7 +183,7 @@
     set_bias(0, mine.astype(F32))
     for load in loads[1:]:
         load.wait()
-    lax.fori_loop(0, 2, alone, 0)
+    lax.fori_loop(0, 1, alone, 0)
     pl.semaphore_wait(barrier, count)
 
     id_copies = [
@@ -197,7 +198,7 @@
         copy.start()
     heard = signal_around(heard_1, "xyz", 1)
 
-    lax.fori_loop(2, 4, alone, 0)
+    lax.fori_loop(1, 2, alone, 0)
     for copy in id_copies:
         copy.wait()
     pl.semaphore_wait(heard_1, heard)
@@ -278,13 +279,13 @@
         copy.start()
         far_copies.append(copy)
 
-    lax.fori_loop(4, HEADS // AT_ONCE, alone, 0)
-    lax.fori_loop(0, HEADS, sum_alone, 0, unroll=2)
+    lax.fori_loop(2, HEADS // ALONE_AT_ONCE, alone, 0)
+    lax.fori_loop(0, HEADS, sum_alone, 0, unroll=4)
 
     def between_cores(step, carry):
         own_rows, other_rows = masks[0] != 0, masks[1] != 0
-        for part in range(AT_ONCE // 2):
-            places = [step * AT_ONCE + part * 2 + h for h in range(2)]
+        for part in range(NEAR_AT_ONCE // 2):
+            places = [step * NEAR_AT_ONCE + part * 2 + h for h in range(2)]
             heads = [core * NEAR_HEADS + place for place in places]
             columns, inner = [head_columns(h) for h in heads], [head_columns(p) for p in places]
             raw = [
@@ -301,7 +302,7 @@
 
     for copy in near_copies:
         copy.wait_recv()
-    lax.fori_loop(0, NEAR_HEADS // AT_ONCE, between_cores, 0)
+    lax.fori_loop(0, NEAR_HEADS // NEAR_AT_ONCE, between_cores, 0)
     near_return = remote(near_out, near_back, near_back_sem, near)
     near_return.start()
 

time: 54.4 us -> 54 us (level)
  no operation moved by 1% of the time
where the time goes in v5:
time: 54 us; the launch traced here: 53.8 us
  Pallas kernels  53 us (98%)
  between operations  0.8 us (1%)
    pallas_call x1, Pallas kernels, per_device(): pl.pallas_call(kernel, out_shape=[vmem((2,) + wide, BF16), vmem((2,) + pa...  51.8 us
    pallas_call x1, Pallas kernels, per_device(): pl.pallas_call(hand_out, out_shape=[jax.ShapeDtypeStruct(wide, BF16), jax...  1.18 us

profile of v5, /device:TPU:2, one launch (start us, length us, event | category | flops | bytes accessed | tf_op | source)
XLA Modules:
  0.0 53.8 jit_solution(15653289078003823427)
XLA Ops:
  0.6 51.8 %shard_map.102 = (bf16[2,128,3072]{2,1,0:T(8,128)(2,1)S(1)}, f32[2,24,128]{2,1,0:T(8,128)S(1)}) custom-call(bf16[128,3072]{1,0:T(8,128)(2,1)} %bitcast.6, bf16[128,3072]{1,0:T(8,128)(2,1)} %bitcast.7, bf16[128,3072]{1,0:T(8,128)(2,1)} %bitcast.8, bf16[128,3072]{1,0:T(8,128)(2,1)} %bitcast.9, s32[1,128]{1,0:T(1,128)} %ids_ref.1, f32[24,128]{1,0:T(8,128)} %gain_q_ref.1, ...), custom_call_target="tpu_custom_call" | custom-call | flops 1610612736 | bytes 5242880 | tf_op jit(solution)/shard_map/pallas_call | solution.py:425
  52.5 1.2 %shard_map.103 = (bf16[128,3072]{1,0:T(8,128)(2,1)}, bf16[128,3072]{1,0:T(8,128)(2,1)}, f32[24,128]{1,0:T(8,128)}, f32[24,128]{1,0:T(8,128)}) custom-call(bf16[2,128,3072]{2,1,0:T(8,128)(2,1)S(1)} %get-tuple-element.10.result, f32[2,24,128]{2,1,0:T(8,128)S(1)} %get-tuple-element.11.sums), custom_call_target="tpu_custom_call" | custom-call | tf_op jit(solution)/shard_map/pallas_call | solution.py:477
